TPU v7x, 32 devices: a whole 2x2x4 slice. The times are simulated.
32 devices in a mesh: dp: 4 (over y, x), expert: 8 (over z, core).
Axes of the slice: x: 2, y: 2, z: 4, core: 2. Of those that a mesh axis runs over, the one named last changes fastest.
Arguments:
- tokens: bfloat16 [1024, 4096], P('expert'), may hold values from -6 to 6
- w_gate: bfloat16 [64, 4096, 1536], P('expert', None, 'dp'), may hold values from -0.09375 to 0.09375
- w_up: bfloat16 [64, 4096, 1536], P('expert', None, 'dp'), may hold values from -0.09375 to 0.09375
- w_down: bfloat16 [64, 1536, 4096], P('expert', 'dp'), may hold values from -0.15625 to 0.15625
- route_ids: int32 [1024, 8], P('expert'), may hold values from 0 to 63, all different within a row; in each aligned block of 128 rows (0 to 127, 128 to 255, ...) at most 24 rows name the same one
- route_weight: float32 [1024, 8], P('expert'), may hold values from 0.1 to 1
Outputs:
- mixed: bfloat16 [1024, 4096], P('expert', 'dp')
Inputs may be any that keep to these rules, and one draw needn't show every extreme that they name: `route_ids`: each row names 8 different experts. Within each aligned block of 128 rows (the rows of one device) no expert is named more than 24 times, and in every draw some expert is named exactly 24 times in some block.
All inputs are finite; a program needn't handle non-finite values.
Results may differ from a plain program's by a relative error of at most 0.013.
Values may be sent and summed in bfloat16 or wider, within the bound.
A program may use at most 256 MiB of HBM per device.

v0:
```python
import jax
import jax.numpy as jnp
from jax import lax
from jax.sharding import PartitionSpec as P

EXPERTS = 64
TOPK = 8


def on_device(tokens, w_gate, w_up, w_down, route_ids, route_weight):
    tok_rows = tokens.shape[0]
    model_width = tokens.shape[1]
    groups = lax.axis_size("dp")
    peer_count = lax.axis_size("expert")
    local_count = w_gate.shape[0]
    capacity = groups * max(1, 3 * tok_rows * TOPK // (2 * EXPERTS * groups))
    flat_ids = route_ids.reshape(-1)
    onehot = (flat_ids[:, None] == jnp.arange(EXPERTS, dtype=jnp.int32)[None, :]).astype(jnp.int32)
    slot_index = jnp.sum((jnp.cumsum(onehot, axis=0) - onehot) * onehot, axis=1)
    target_row = flat_ids * capacity + slot_index
    owner_token = jnp.repeat(jnp.arange(tok_rows, dtype=jnp.int32), TOPK)
    source_token = (
        jnp.full((EXPERTS * capacity,), tok_rows, jnp.int32).at[target_row].set(owner_token)
    )
    padded = jnp.concatenate([tokens, jnp.zeros((1, model_width), tokens.dtype)], axis=0)
    outgoing = padded[source_token].reshape(EXPERTS, capacity, model_width)
    arrived = lax.all_to_all(outgoing, "expert", split_axis=0, concat_axis=0, tiled=True)
    expert_rows = arrived.reshape(peer_count, local_count, capacity, model_width)
    gate_proj = jnp.einsum(
        "slcd,ldh->slch", expert_rows, w_gate, preferred_element_type=jnp.float32
    )
    up_proj = jnp.einsum("slcd,ldh->slch", expert_rows, w_up, preferred_element_type=jnp.float32)
    hidden = (jax.nn.silu(gate_proj) * up_proj).astype(jnp.bfloat16)
    partial_value = jnp.einsum(
        "slch,lhd->slcd", hidden, w_down, preferred_element_type=jnp.float32
    ).astype(jnp.bfloat16)
    partial_value = partial_value.reshape(peer_count * local_count, capacity, model_width)
    returned = lax.all_to_all(partial_value, "expert", split_axis=0, concat_axis=0, tiled=True)
    picked = returned.reshape(EXPERTS * capacity, model_width)[target_row].reshape(
        tok_rows, TOPK, model_width
    )
    mixed_rows = jnp.sum(route_weight[:, :, None] * picked.astype(jnp.float32), axis=1)
    return lax.psum_scatter(mixed_rows.astype(jnp.bfloat16), "dp", scatter_dimension=1, tiled=True)


def solution(mesh):
    return jax.shard_map(
        on_device,
        mesh=mesh,
        in_specs=(
            P("expert", None),
            P("expert", None, "dp"),
            P("expert", None, "dp"),
            P("expert", "dp", None),
            P("expert", None),
            P("expert", None),
        ),
        out_specs=P("expert", "dp"),
        check_vma=False,
    )
```

profile of v0, /device:TPU:0, one launch (start us, length us, event | category | flops | bytes accessed | tf_op | source)
XLA Modules:
  0.0 724.7 jit_solution(170659015018113271)
XLA Ops:
  6.5 0.8 copy.10
  7.3 0.1 eq.29
  7.4 0.1 eq.25
  7.5 0.7 broadcast_multiply_fusion
  8.2 18.0 %reduce-window.6 = s32[64,8,128]{2,1,0:T(8,128)S(1)} reduce-window(s32[64,8,128]{2,1,0:T(8,128)S(1)} %fusion.27, s32[]{:T(128)} %constant.11.clone.1), window={size=1x1x128 pad=0_0x0_0x127_0}, to_apply=%region_0.0 | reduce-window | flops 8323072 | bytes 524292 | tf_op jit(solution)/shard_map/reduce-window
  26.2 0.1 slice.12
  26.4 0.1 copy.12
  26.6 0.1 broadcast_add_fusion
  26.8 0.1 copy.9
  26.9 0.1 mul.37
  27.2 4.3 scatter_custom_fusion
  31.5 1.3 concatenate.3
  32.9 9.6 %gather_fusion = bf16[1536,4096]{1,0:T(8,128)(2,1)} fusion(bf16[129,4096]{1,0:T(8,128)(2,1)S(1)} %concatenate.3, s32[2048]{0:T(1024)S(1)} %pad_clamp_fusion), kind=kCustom, calls=%fused_computation | custom fusion | bytes 25171968 | tf_op jit(solution)/shard_map/gather | solution.py:26
  42.5 281.3 %all_to_all.10 = bf16[64,24,4096]{2,1,0:T(8,128)(2,1)} all-to-all(bf16[64,24,4096]{2,1,0:T(8,128)(2,1)} %bitcast.71), channel_id=1, replica_groups=mesh['dp'=4,'expert'=8] {'expert'}, dimensions={0} | all-to-all | bytes 25165824 | tf_op jit(solution)/shard_map/all_to_all | solution.py:27
  323.8 15.4 %fusion.2 = f32[8,8,24,384]{3,2,1,0:T(8,128)S(1)} fusion(bf16[8,4096,384]{2,1,0:T(8,128)(2,1)} %param.8, bf16[8,8,24,4096]{3,2,1,0:T(8,128)(2,1)} %bitcast.73), kind=kOutput, calls=%fused_computation.5 | convolution fusion | flops 4831838208 | bytes 40108032 | tf_op jit(solution)/shard_map/slcd,ldh->slch/dot_general | solution.py:32
  339.2 26.5 %convert_bitcast_fusion = bf16[8,8,24,4096]{3,2,0,1:T(8,128)(2,1)} fusion(bf16[8,384,4096]{2,1,0:T(8,128)(2,1)} %param.9, f32[8,8,24,384]{3,2,1,0:T(8,128)S(1)} %fusion.2, bf16[8,4096,384]{2,1,0:T(8,128)(2,1)} %param.7, bf16[8,8,24,4096]{3,2,1,0:T(8,128)(2,1)} %bitcast.74), kind=kOutput, calls=%fused_computation.11 | convolution fusion | flops 9673506816 | bytes 77856768 | tf_op jit(solution)/shard_map/slch,lhd->slcd/dot_general | solution.py:34
  365.8 10.7 %copy.15 = bf16[8,8,24,4096]{3,2,1,0:T(8,128)(2,1)} copy(bf16[8,8,24,4096]{3,2,0,1:T(8,128)(2,1)} %convert_bitcast_fusion) | data formatting | bytes 25165824 | tf_op jit(solution)/shard_map/convert_element_type | solution.py:36
  376.5 5.5 all-to-all-start.1
  381.9 0.2 reduce-scatter.2.cloned.1.call-start
  382.2 0.1 copy.8
  382.3 273.4 %all-to-all-done.1 = bf16[64,24,4096]{2,1,0:T(8,128)(2,1)} async-done(((bf16[64,24,4096]{2,1,0:T(8,128)(2,1)}), bf16[64,24,4096]{2,1,0:T(8,128)(2,1)}, u32[]{:S(2)}, u32[]{:S(2)}) %all-to-all-start.1) | async-done | bytes 12582944 | tf_op jit(solution)/shard_map/all_to_all | solution.py:38
  655.7 21.3 %gather_fusion.1 = bf16[1024,4096]{1,0:T(8,128)(2,1)} fusion(bf16[1536,4096]{1,0:T(8,128)(2,1)} %bitcast.16, s32[1024]{0:T(1024)S(1)} %broadcast_clamp_fusion), kind=kCustom, calls=%fused_computation.1 | custom fusion | bytes 16781312 | tf_op jit(solution)/shard_map/gather | solution.py:39
  677.0 12.9 %fusion.6 = bf16[128,4096]{1,0:T(8,128)(2,1)} fusion(bf16[1024,4096]{1,0:T(8,128)(2,1)} %gather_fusion.1, f32[128,8]{1,0:T(8,128)S(1)} %copy.8), kind=kLoop, calls=%fused_computation.10 | loop fusion | flops 12058624 | bytes 9441280 | tf_op jit(solution)/shard_map/reduce_sum | solution.py:42
  689.9 27.9 %reduce-scatter.2.cloned.1.call-done = bf16[128,1024]{1,0:T(8,128)(2,1)} async-done(((bf16[128,4096]{1,0:T(8,128)(2,1)}), bf16[128,1024]{1,0:T(8,128)(2,1)}) %reduce-scatter.2.cloned.1.call-update) | async-done | bytes 262160 | tf_op jit(solution)/shard_map/reduce_scatter | solution.py:43
  (14 shorter events, 0.3 us)
Async XLA Ops:
  376.5 5.7 copy-start
  376.5 279.3 %all-to-all-start.1 = ((bf16[64,24,4096]{2,1,0:T(8,128)(2,1)}), bf16[64,24,4096]{2,1,0:T(8,128)(2,1)}, u32[]{:S(2)}, u32[]{:S(2)}) async-start(bf16[64,24,4096]{2,1,0:T(8,128)(2,1)} %bitcast.72), calls=%async_computation.1 | async-start | bytes 25165824 | tf_op jit(solution)/shard_map/all_to_all | solution.py:38
  381.9 335.9 %reduce-scatter.2.cloned.1.call-start = ((), (), s32[]{:S(2)}) async-start(), calls=%async_computation.3 | async-start | bytes 1310720 | tf_op jit(solution)/shard_map/reduce_scatter | solution.py:43
Sparse Core Ops, SparseCore 0:
  690.0 27.7 reduce-scatter.1
where the time goes:
time: 725 us
  waiting for transfers between devices  301 us (42%)
  blocking collectives  281 us (39%)
  local copies, waits for them, and re-layouts  48.9 us (7%)
  matrix products  42 us (6%)
  other arithmetic  31.9 us (4%)
  between operations  13.5 us (2%)
    all_to_all x1, blocking collectives, on_device(): lax.all_to_all(outgoing, 'expert', split_axis=0, concat_axis=0, tiled=True)  281 us
    all_to_all x1, waiting for transfers between devices, on_device(): lax.all_to_all(partial_value, 'expert', split_axis=0, concat_axis=0, tile...  273 us
    reduce_scatter x1, waiting for transfers between devices, on_device(): lax.psum_scatter(mixed_rows.astype(jnp.bfloat16), 'dp', scatter_dimension...  27.9 us
    dot_general x1, matrix products, on_device(): jnp.einsum('slch,lhd->slcd', hidden, w_down, preferred_element_type=jnp.f...  26.5 us
    gather x1, local copies, waits for them, and re-layouts, on_device(): returned.reshape(EXPERTS * capacity, model_width)[target_row]  21.3 us
    another operation x3, other arithmetic  18.2 us
    dot_general x1, matrix products, on_device(): jnp.einsum('slcd,ldh->slch', expert_rows, w_up, preferred_element_type=jn...  15.4 us
  transfers between devices with their start and end apart: 2, of which 2 were waited for; matrix products, arithmetic and copies ran while one was open for 0% of the time, Pallas kernels for 0%

commit v1 on v0

--- a/solution.py
+++ b/solution.py
@@ -1,13 +1,17 @@
 import jax
 import jax.numpy as jnp
 from jax import lax
+from jax.experimental import pallas as pl
+from jax.experimental.pallas import tpu as pltpu
 from jax.sharding import PartitionSpec as P
 
 EXPERTS = 64
 TOPK = 8
-
-
-def on_device(tokens, w_gate, w_up, w_down, route_ids, route_weight):
+CAP = 24
+MESH = pl.DeviceIdType.MESH
+
+
+def general(tokens, w_gate, w_up, w_down, route_ids, route_weight):
     tok_rows = tokens.shape[0]
     model_width = tokens.shape[1]
     groups = lax.axis_size("dp")
@@ -43,9 +47,340 @@
     return lax.psum_scatter(mixed_rows.astype(jnp.bfloat16), "dp", scatter_dimension=1, tiled=True)
 
 
+def kernel(
+    toks, meta, wg, wu, wd, out,
+    tok, met, pick, put, rows, rw, hid, gu, dn, down, res, sib, xin, yin, zin,
+    tok_r, z_s, sib_s, fx_s, fy_s, rl_s, met_s, met_r, gu_m, dn_m,
+    back_s, back_r, x_s, x_r, y_s, y_r, zz_s, zz_r,
+):
+    n_loc, _, hpart = wg.shape
+    tb = toks.shape[0]
+    wide = toks.shape[1] // 4
+    pair = 2 * CAP
+    half = wide // 2
+    q = lax.axis_index("dp")
+    ex = lax.axis_index("expert")
+    z, c = ex // 2, ex % 2
+    y, x = q // 2, q % 2
+    qx = y * 2 + (1 - x)
+    qy = (1 - y) * 2 + x
+    qd = 3 - q
+    chunk = {0: q, 1: qx, 2: qy, 3: qd}
+    other = 1 - c
+    twin = z * 2 + other
+
+    def remote(src, dst, s, r, dp, e):
+        return pltpu.make_async_remote_copy(
+            src_ref=src, dst_ref=dst, send_sem=s, recv_sem=r,
+            device_id=(dp, e), device_id_type=MESH,
+        )
+
+    def cols(j):
+        return pl.ds(pl.multiple_of(j * wide, wide), wide)
+
+    def gu_copy(e, slot):
+        return (
+            pltpu.make_async_copy(wg.at[e], gu.at[slot, 0], gu_m.at[slot, 0]),
+            pltpu.make_async_copy(wu.at[e], gu.at[slot, 1], gu_m.at[slot, 1]),
+        )
+
+    order = (3, 1, 2, 0)
+
+    def dn_copy(step):
+        col = chunk[order[step // 2]] * wide + (step % 2) * half
+        slot = step % 2
+        return pltpu.make_async_copy(
+            wd.at[:, :, pl.ds(pl.multiple_of(col, half), half)], dn.at[slot], dn_m.at[slot]
+        )
+
+    barrier = pltpu.get_barrier_semaphore()
+    for k in range(1, 8):
+        pl.semaphore_signal(barrier, inc=1, device_id=(q, (ex + k) % 8), device_id_type=MESH)
+    for peer in (qx, qy):
+        pl.semaphore_signal(barrier, inc=1, device_id=(peer, ex), device_id_type=MESH)
+    pl.semaphore_wait(barrier, 9)
+
+    sends = []
+
+    for dz in (1, 2, 3):
+        cp = remote(toks.at[:, cols(q)], tok.at[q, ex], z_s.at[dz - 1], tok_r.at[q, ex],
+                    q, ((z + dz) % 4) * 2 + c)
+        cp.start()
+        sends.append(cp)
+    for k in range(1, 8):
+        cp = remote(meta, met.at[ex], met_s.at[k - 1], met_r.at[ex], q, (ex + k) % 8)
+        cp.start()
+        sends.append(cp)
+    own_meta = pltpu.make_async_copy(meta, met.at[ex], met_r.at[ex])
+    own_meta.start()
+    own = []
+    for j in range(4):
+        cp = pltpu.make_async_copy(toks.at[:, pl.ds(j * wide, wide)], tok.at[j, ex],
+                                   tok_r.at[j, ex])
+        cp.start()
+        own.append(cp)
+        cp = remote(toks.at[:, pl.ds(j * wide, wide)], tok.at[j, ex], sib_s.at[j, 0],
+                    tok_r.at[j, ex], q, twin)
+        cp.start()
+        sends.append(cp)
+    for e in range(2):
+        for cp in gu_copy(e, e):
+            cp.start()
+    for step in range(2):
+        dn_copy(step).start()
+
+    def arrive(j, s):
+        remote(tok.at[j, s], tok.at[j, s], z_s.at[0], tok_r.at[j, s], q, twin).wait_recv()
+
+    def forward(j, s, sem, dp, e):
+        cp = remote(tok.at[j, s], tok.at[j, s], sem, tok_r.at[j, s], dp, e)
+        cp.start()
+        sends.append(cp)
+
+    for dz in (1, 2, 3):
+        s = ((z + 4 - dz) % 4) * 2 + c
+        arrive(q, s)
+        forward(q, s, fx_s.at[dz - 1], qx, ex)
+        forward(q, s, fy_s.at[dz - 1], qy, ex)
+        forward(q, s, sib_s.at[0, dz], q, twin)
+    rel_in = qx * (1 - c) + qy * c
+    rel_out = qy * (1 - c) + qx * c
+
+    own_meta.wait()
+    for k in range(1, 8):
+        s = (ex + k) % 8
+        remote(meta, met.at[s], met_s.at[0], met_r.at[s], q, twin).wait_recv()
+    before = (
+        lax.broadcasted_iota(jnp.int32, (tb, tb), 0) < lax.broadcasted_iota(jnp.int32, (tb, tb), 1)
+    ).astype(jnp.bfloat16)
+    spot = lax.broadcasted_iota(jnp.int32, (n_loc, pair, 2 * tb), 1).astype(jnp.float32)
+
+    def build(p, carry):
+        vals, wts = [], []
+        for k in range(2):
+            ids = met[2 * p + k, 0:TOPK]
+            wt = met[2 * p + k, TOPK:2 * TOPK]
+            ms, ws = [], []
+            for e in range(n_loc):
+                eq = ids == (ex * n_loc + e).astype(jnp.float32)
+                ms.append(jnp.sum(jnp.where(eq, 1.0, 0.0), axis=0, keepdims=True))
+                ws.append(jnp.sum(jnp.where(eq, wt, 0.0), axis=0, keepdims=True))
+            m = jnp.concatenate(ms, axis=0)
+            slot = jnp.dot(m.astype(jnp.bfloat16), before, preferred_element_type=jnp.float32)
+            vals.append(jnp.where(m > 0.5, slot + float(CAP * k), -1.0))
+            wts.append(jnp.concatenate(ws, axis=0))
+        val = jnp.concatenate(vals, axis=1)
+        wgt = jnp.concatenate(wts, axis=1)
+        hot = jnp.where(val[:, None, :] == spot, 1.0, 0.0)
+        rw[:, pl.ds(pl.multiple_of(p * pair, 16), pair), :] = jnp.sum(
+            hot * wgt[:, None, :], axis=2, keepdims=True
+        )
+        hot = hot.reshape(n_loc * pair, 2 * tb)
+        pick[p] = hot.astype(jnp.bfloat16)
+        put[p] = hot.T.astype(jnp.bfloat16)
+        return carry
+
+    lax.fori_loop(0, 4, build, 0)
+
+    for dz in (1, 2, 3):
+        s = ((z + 4 - dz) % 4) * 2 + c
+        arrive(rel_in, s)
+        forward(rel_in, s, rl_s.at[dz - 1], rel_out, ex)
+        forward(rel_in, s, sib_s.at[1, dz], q, twin)
+        arrive(rel_out, s)
+        forward(rel_out, s, sib_s.at[2, dz], q, twin)
+    for dz in (1, 2, 3):
+        s = ((z + 4 - dz) % 4) * 2 + c
+        arrive(qd, s)
+        forward(qd, s, sib_s.at[3, dz], q, twin)
+    for cp in own:
+        cp.wait()
+
+    def fill(i, carry):
+        p, j = i // 4, i % 4
+        block = tok[j, pl.ds(2 * p, 2)].reshape(2 * tb, wide)
+        got = jnp.dot(pick[p], block, preferred_element_type=jnp.float32).astype(jnp.bfloat16)
+        rows[:, pl.ds(pl.multiple_of(p * pair, 16), pair), cols(j)] = got.reshape(
+            n_loc, pair, wide
+        )
+        return carry
+
+    for dz in range(4):
+        s = ((z + 4 - dz) % 4) * 2 + other
+        for j in range(4):
+            arrive(j, s)
+    lax.fori_loop(0, 16, fill, 0)
+
+    def up(e, carry):
+        slot = e % 2
+        for cp in gu_copy(e, slot):
+            cp.wait()
+        a = rows[e]
+        g = jnp.dot(a, gu[slot, 0], preferred_element_type=jnp.float32)
+        u = jnp.dot(a, gu[slot, 1], preferred_element_type=jnp.float32)
+        h = g / (1.0 + jnp.exp(-g)) * u * rw[e]
+        hid[e] = h.astype(jnp.bfloat16)
+
+        @pl.when(e + 2 < n_loc)
+        def _():
+            for cp in gu_copy(e + 2, slot):
+                cp.start()
+
+        return carry
+
+    lax.fori_loop(0, n_loc, up, 0)
+
+    def project(step):
+        slot = step % 2
+        d = order[step // 2]
+        dn_copy(step).wait()
+
+        def one(e, carry):
+            v = jnp.dot(hid[e], dn[slot, e], preferred_element_type=jnp.float32)
+            v = v.astype(jnp.bfloat16).reshape(4, pair, half)
+            down[:, pl.ds(pl.multiple_of(e * pair, 16), pair), :] = v
+            return carry
+
+        lax.fori_loop(0, n_loc, one, 0)
+        if step + 2 < 8:
+            dn_copy(step + 2).start()
+
+        def spread(p, carry):
+            v = jnp.dot(put[p], down[p], preferred_element_type=jnp.float32).astype(jnp.bfloat16)
+            v = v.reshape(2, tb, half)
+            res[d, :, p, :, pl.ds((step % 2) * half, half)] = v
+            return carry
+
+        lax.fori_loop(0, 4, spread, 0)
+
+    def back(d, p):
+        return remote(res.at[d, other, p], sib.at[d, p], back_s.at[d, p], back_r.at[d, p],
+                      q, twin)
+
+    def over_x(d, p, slot):
+        return remote(res.at[d, c, p], xin.at[slot, p % 2], x_s.at[slot, p % 2],
+                      x_r.at[slot, p % 2], qx, ex)
+
+    def over_y(d, p, slot):
+        return remote(res.at[d, c, p], yin.at[slot, p % 2], y_s.at[slot, p % 2],
+                      y_r.at[slot, p % 2], qy, ex)
+
+    def add(d, p, terms):
+        total = res[d, c, p].astype(jnp.float32)
+        for t in terms:
+            total = total + t[...].astype(jnp.float32)
+        return total
+
+    def with_twin(d, p, extra=()):
+        back(d, p).wait_recv()
+        res[d, c, p] = add(d, p, (sib.at[d, p],) + tuple(extra)).astype(jnp.bfloat16)
+
+    def go(cp):
+        cp.start()
+        sends.append(cp)
+
+    def stage(d):
+        if d == 3:
+            for p in (0, 2, 1, 3):
+                with_twin(3, p)
+                go(over_x(3, p, 0) if p < 2 else over_y(3, p, 0))
+        if d == 1:
+            for p in (0, 1):
+                with_twin(1, p)
+                go(over_x(1, p, 1))
+        if d == 2:
+            for p in (2, 3):
+                with_twin(2, p)
+                go(over_y(2, p, 1))
+
+    for i, d in enumerate(order):
+        project(2 * i)
+        project(2 * i + 1)
+        for p in range(4):
+            go(back(d, p))
+        if i >= 1:
+            stage(order[i - 1])
+
+    for k in range(2):
+        over_x(3, k, 0).wait_recv()
+        with_twin(2, k, (xin.at[0, k],))
+        go(over_y(2, k, 2))
+        over_y(3, 2 + k, 0).wait_recv()
+        with_twin(1, 2 + k, (yin.at[0, k],))
+        go(over_x(1, 2 + k, 2))
+
+    for p in range(4):
+        back(0, p).wait_recv()
+    for dz in (2, 1, 3, 0):
+        p = (z + dz) % 4
+        h, k = p // 2, p % 2
+        remote(xin.at[1 + h, k], xin.at[1 + h, k], x_s.at[0, 0], x_r.at[1 + h, k],
+               qx, ex).wait_recv()
+        remote(yin.at[2 - h, k], yin.at[2 - h, k], y_s.at[0, 0], y_r.at[2 - h, k],
+               qy, ex).wait_recv()
+        total = add(0, p, (sib.at[0, p], xin.at[1 + h, k], yin.at[2 - h, k]))
+        if dz:
+            res[0, c, p] = total.astype(jnp.bfloat16)
+            go(remote(res.at[0, c, p], zin.at[dz - 1], zz_s.at[dz - 1], zz_r.at[dz - 1],
+                      q, p * 2 + c))
+    for dz in (1, 2, 3):
+        remote(zin.at[dz - 1], zin.at[dz - 1], zz_s.at[0], zz_r.at[dz - 1], q, twin).wait_recv()
+        total = total + zin[dz - 1].astype(jnp.float32)
+    out[...] = total.astype(jnp.bfloat16)
+    for cp in sends:
+        cp.wait_send()
+
+
+def fused(tokens, w_gate, w_up, w_down, route_ids, route_weight):
+    tb, width = tokens.shape
+    n_loc, _, hpart = w_gate.shape
+    wide = width // 4
+    half = wide // 2
+    bf, f32 = jnp.bfloat16, jnp.float32
+    meta = jnp.concatenate([route_ids.astype(f32).T, route_weight.T], axis=0)
+    dma = pltpu.SemaphoreType.DMA
+    r = 8 * CAP
+    hbm = pl.BlockSpec(memory_space=pl.ANY)
+    return pl.pallas_call(
+        kernel,
+        out_shape=jax.ShapeDtypeStruct((tb, wide), bf),
+        in_specs=[hbm, pl.BlockSpec(memory_space=pltpu.VMEM), hbm, hbm, hbm],
+        out_specs=pl.BlockSpec(memory_space=pltpu.VMEM),
+        scratch_shapes=[
+            pltpu.VMEM((4, 8, tb, wide), bf),
+            pltpu.VMEM((8, 2 * TOPK, tb), f32),
+            pltpu.VMEM((4, n_loc * 2 * CAP, 2 * tb), bf),
+            pltpu.VMEM((4, 2 * tb, n_loc * 2 * CAP), bf),
+            pltpu.VMEM((n_loc, r, width), bf),
+            pltpu.VMEM((n_loc, r, 1), f32),
+            pltpu.VMEM((n_loc, r, hpart), bf),
+            pltpu.VMEM((2, 2, width, hpart), bf),
+            pltpu.VMEM((2, n_loc, hpart, half), bf),
+            pltpu.VMEM((4, n_loc * 2 * CAP, half), bf),
+            pltpu.VMEM((4, 2, 4, tb, wide), bf),
+            pltpu.VMEM((4, 4, tb, wide), bf),
+            pltpu.VMEM((3, 2, tb, wide), bf),
+            pltpu.VMEM((3, 2, tb, wide), bf),
+            pltpu.VMEM((3, tb, wide), bf),
+            dma((4, 8)), dma((3,)), dma((4, 4)), dma((3,)), dma((3,)), dma((3,)),
+            dma((7,)), dma((8,)), dma((2, 2)), dma((2,)),
+            dma((4, 4)), dma((4, 4)), dma((3, 2)), dma((3, 2)), dma((3, 2)), dma((3, 2)),
+            dma((3,)), dma((3,)),
+        ],
+        compiler_params=pltpu.CompilerParams(
+            collective_id=0, has_side_effects=True, vmem_limit_bytes=63 * 1024 * 1024
+        ),
+        cost_estimate=pl.CostEstimate(
+            flops=20_000_000_000, bytes_accessed=80_000_000, transcendentals=0
+        ),
+        name="moe",
+    )(tokens, meta, w_gate, w_up, w_down)
+
+
 def solution(mesh):
+    small = mesh.shape["dp"] == 4 and mesh.shape["expert"] == 8
     return jax.shard_map(
-        on_device,
+        fused if small else general,
         mesh=mesh,
         in_specs=(
             P("expert", None),

time: 725 us -> 151 us (0.21)
  waiting for transfers between devices: 301 us -> 0 us
  blocking collectives: 281 us -> 0 us
  Pallas kernels: 0 us -> 146 us
  local copies, waits for them, and re-layouts: 48.9 us -> 1.67 us
  matrix products: 42 us -> 0 us
  other arithmetic: 31.9 us -> 1.97 us
  between operations: 13.5 us -> 0.01 us
    all_to_all x1 -> x0, blocking collectives: 281 us -> none  [on_device(): lax.all_to_all(outgoing, 'expert', split_axis=0, concat_axis=0, tiled=True)]
    all_to_all x1 -> x0, waiting for transfers between devices: 273 us -> none  [on_device(): lax.all_to_all(partial_value, 'expert', split_axis=0, concat_axis=0, tile...]
    pallas_call x0 -> x1, Pallas kernels: none -> 146 us  [fused(): pl.pallas_call(kernel, out_shape=jax.ShapeDtypeStruct((tb, wide), bf), in...]
    dot_general x2 -> x0, matrix products: 42 us -> none  [the longest x1 26.5 us: on_device(): jnp.einsum('slch,lhd->slcd', hidden, w_down, preferred_element_type=jnp.f...]
    gather x2 -> x0, local copies, waits for them, and re-layouts: 30.9 us -> none  [the longest x1 21.3 us: on_device(): returned.reshape(EXPERTS * capacity, model_width)[target_row]]
    reduce_scatter x1 -> x0, waiting for transfers between devices: 27.9 us -> none  [on_device(): lax.psum_scatter(mixed_rows.astype(jnp.bfloat16), 'dp', scatter_dimension...]
    another operation x3 -> x0, other arithmetic: 18.2 us -> none
    reduce_sum x2 -> x0, other arithmetic: 13 us -> none  [the longest x1 12.9 us: on_device(): jnp.sum(route_weight[:, :, None] * picked.astype(jnp.float32), axis=1)]
  transfers between devices with their start and end apart: 2 -> 0, of which waited for: 2 -> 0; matrix products, arithmetic and copies ran while one was open for 0% -> 0% of each run, Pallas kernels for 0% -> 0%
where the time goes in v1:
time: 151 us; the launch traced here: 150 us
  Pallas kernels  146 us (97%)
  other arithmetic  1.97 us (1%)
  local copies, waits for them, and re-layouts  1.67 us (1%)
    pallas_call x1, Pallas kernels, fused(): pl.pallas_call(kernel, out_shape=jax.ShapeDtypeStruct((tb, wide), bf), in...  146 us

profile of v1, /device:TPU:0, one launch (start us, length us, event | category | flops | bytes accessed | tf_op | source)
XLA Modules:
  0.0 149.6 jit_solution(293154950370264524)
XLA Ops:
  0.0 0.7 convert_bitcast_fusion
  0.7 1.3 pad_maximum_fusion.meta
  2.0 145.9 %moe.1 = bf16[128,1024]{1,0:T(8,128)(2,1)} custom-call(bf16[128,4096]{1,0:T(8,128)(2,1)} %toks.1, f32[16,128]{1,0:T(8,128)} %pad_maximum_fusion.meta, bf16[8,4096,384]{2,1,0:T(8,128)(2,1)} %wg.1, bf16[8,4096,384]{2,1,0:T(8,128)(2,1)} %wu.1, bf16[8,384,4096]{2,1,0:T(8,128)(2,1)} %wd.1), custom_call_target="tpu_custom_call" | custom-call | flops 20000000000 | bytes 80000000 | tf_op jit(solution)/shard_map/moe/pallas_call | solution.py:344
  147.9 1.7 %copy.8 = bf16[128,1024]{1,0:T(8,128)(2,1)} copy(bf16[128,1024]{1,0:T(8,128)(2,1)} %moe.1) | data formatting | bytes 524288

commit v2 on v1

--- a/solution.py
+++ b/solution.py
@@ -102,15 +102,25 @@
 
     sends = []
 
-    for dz in (1, 2, 3):
-        cp = remote(toks.at[:, cols(q)], tok.at[q, ex], z_s.at[dz - 1], tok_r.at[q, ex],
-                    q, ((z + dz) % 4) * 2 + c)
-        cp.start()
-        sends.append(cp)
+    top = z // 2
+    source = (top * 2 + 1 - z % 2, 2 - top, 3 - 3 * top)
+    inner = z + 1 - 2 * top
+    outer = (z + 3 + 2 * top) % 4
+    middle = inner + z == 3
     for k in range(1, 8):
         cp = remote(meta, met.at[ex], met_s.at[k - 1], met_r.at[ex], q, (ex + k) % 8)
         cp.start()
         sends.append(cp)
+    cp = remote(toks.at[:, cols(q)], tok.at[q, ex], z_s.at[3], tok_r.at[q, ex], q, inner * 2 + c)
+    cp.start()
+    sends.append(cp)
+    outward = remote(toks.at[:, cols(q)], tok.at[q, ex], z_s.at[4], tok_r.at[q, ex],
+                     q, outer * 2 + c)
+
+    @pl.when(middle)
+    def _():
+        outward.start()
+
     own_meta = pltpu.make_async_copy(meta, met.at[ex], met_r.at[ex])
     own_meta.start()
     own = []
@@ -137,12 +147,23 @@
         cp.start()
         sends.append(cp)
 
-    for dz in (1, 2, 3):
-        s = ((z + 4 - dz) % 4) * 2 + c
+    passed = []
+
+    def from_line(n):
+        s = source[n] * 2 + c
         arrive(q, s)
-        forward(q, s, fx_s.at[dz - 1], qx, ex)
-        forward(q, s, fy_s.at[dz - 1], qy, ex)
-        forward(q, s, sib_s.at[0, dz], q, twin)
+        cp = remote(tok.at[q, s], tok.at[q, s], z_s.at[n], tok_r.at[q, s],
+                    q, (outer if n else inner) * 2 + c)
+
+        @pl.when(middle)
+        def _():
+            cp.start()
+
+        passed.append(cp)
+        forward(q, s, fx_s.at[n], qx, ex)
+        forward(q, s, fy_s.at[n], qy, ex)
+        forward(q, s, sib_s.at[0, n + 1], q, twin)
+
     rel_in = qx * (1 - c) + qy * c
     rel_out = qy * (1 - c) + qx * c
 
@@ -180,36 +201,50 @@
         put[p] = hot.T.astype(jnp.bfloat16)
         return carry
 
+    from_line(0)
     lax.fori_loop(0, 4, build, 0)
 
-    for dz in (1, 2, 3):
-        s = ((z + 4 - dz) % 4) * 2 + c
+    def from_plane(n):
+        s = source[n] * 2 + c
         arrive(rel_in, s)
-        forward(rel_in, s, rl_s.at[dz - 1], rel_out, ex)
-        forward(rel_in, s, sib_s.at[1, dz], q, twin)
+        forward(rel_in, s, rl_s.at[n], rel_out, ex)
+        forward(rel_in, s, sib_s.at[1, n + 1], q, twin)
         arrive(rel_out, s)
-        forward(rel_out, s, sib_s.at[2, dz], q, twin)
-    for dz in (1, 2, 3):
-        s = ((z + 4 - dz) % 4) * 2 + c
+        forward(rel_out, s, sib_s.at[2, n + 1], q, twin)
+
+    def from_corner(n):
+        s = source[n] * 2 + c
         arrive(qd, s)
-        forward(qd, s, sib_s.at[3, dz], q, twin)
+        forward(qd, s, sib_s.at[3, n + 1], q, twin)
+
+    def fill(p):
+        for j in range(4):
+            arrive(j, p * 2 + other)
+
+        def one(j, carry):
+            block = tok[j, pl.ds(2 * p, 2)].reshape(2 * tb, wide)
+            got = jnp.dot(pick[p], block, preferred_element_type=jnp.float32)
+            rows[:, pl.ds(pl.multiple_of(p * pair, 16), pair), cols(j)] = got.astype(
+                jnp.bfloat16
+            ).reshape(n_loc, pair, wide)
+            return carry
+
+        lax.fori_loop(0, 4, one, 0)
+
+    from_line(1)
+    from_plane(0)
     for cp in own:
         cp.wait()
-
-    def fill(i, carry):
-        p, j = i // 4, i % 4
-        block = tok[j, pl.ds(2 * p, 2)].reshape(2 * tb, wide)
-        got = jnp.dot(pick[p], block, preferred_element_type=jnp.float32).astype(jnp.bfloat16)
-        rows[:, pl.ds(pl.multiple_of(p * pair, 16), pair), cols(j)] = got.reshape(
-            n_loc, pair, wide
-        )
-        return carry
-
-    for dz in range(4):
-        s = ((z + 4 - dz) % 4) * 2 + other
-        for j in range(4):
-            arrive(j, s)
-    lax.fori_loop(0, 16, fill, 0)
+    fill(z)
+    from_line(2)
+    from_plane(1)
+    from_corner(0)
+    from_plane(2)
+    fill(source[0])
+    from_corner(1)
+    from_corner(2)
+    fill(source[1])
+    fill(source[2])
 
     def up(e, carry):
         slot = e % 2
@@ -279,56 +314,80 @@
         cp.start()
         sends.append(cp)
 
-    def stage(d):
-        if d == 3:
-            for p in (0, 2, 1, 3):
-                with_twin(3, p)
-                go(over_x(3, p, 0) if p < 2 else over_y(3, p, 0))
-        if d == 1:
-            for p in (0, 1):
-                with_twin(1, p)
-                go(over_x(1, p, 1))
-        if d == 2:
-            for p in (2, 3):
-                with_twin(2, p)
-                go(over_y(2, p, 1))
-
+    def first_leg(d, p):
+        with_twin(d, p)
+        slot = 0 if d == 3 else 1
+        go(over_x(d, p, slot) if p < 2 else over_y(d, p, slot))
+
+    def second_leg(p):
+        k = p % 2
+        if p < 2:
+            over_x(3, p, 0).wait_recv()
+            with_twin(2, p, (xin.at[0, k],))
+            go(over_y(2, p, 2))
+        else:
+            over_y(3, p, 0).wait_recv()
+            with_twin(1, p, (yin.at[0, k],))
+            go(over_x(1, p, 2))
+
+    def finish(p):
+        k = p % 2
+        last_x, last_y = (1, 2) if p < 2 else (2, 1)
+        over_x(0, p, last_x).wait_recv()
+        over_y(0, p, last_y).wait_recv()
+        with_twin(0, p, (xin.at[last_x, k], yin.at[last_y, k]))
+        slot = (z + 3 - p) % 4
+        cp = remote(res.at[0, c, p], zin.at[slot % 3], zz_s.at[p], zz_r.at[slot % 3], q, p * 2 + c)
+
+        @pl.when(z != p)
+        def _():
+            cp.start()
+
+        ends.append((p, cp))
+
+    ends = []
+    early, late = (0, 3), (1, 2)
     for i, d in enumerate(order):
         project(2 * i)
         project(2 * i + 1)
-        for p in range(4):
+        for p in (0, 3, 1, 2):
             go(back(d, p))
-        if i >= 1:
-            stage(order[i - 1])
-
-    for k in range(2):
-        over_x(3, k, 0).wait_recv()
-        with_twin(2, k, (xin.at[0, k],))
-        go(over_y(2, k, 2))
-        over_y(3, 2 + k, 0).wait_recv()
-        with_twin(1, 2 + k, (yin.at[0, k],))
-        go(over_x(1, 2 + k, 2))
-
-    for p in range(4):
-        back(0, p).wait_recv()
-    for dz in (2, 1, 3, 0):
-        p = (z + dz) % 4
-        h, k = p // 2, p % 2
-        remote(xin.at[1 + h, k], xin.at[1 + h, k], x_s.at[0, 0], x_r.at[1 + h, k],
-               qx, ex).wait_recv()
-        remote(yin.at[2 - h, k], yin.at[2 - h, k], y_s.at[0, 0], y_r.at[2 - h, k],
-               qy, ex).wait_recv()
-        total = add(0, p, (sib.at[0, p], xin.at[1 + h, k], yin.at[2 - h, k]))
-        if dz:
-            res[0, c, p] = total.astype(jnp.bfloat16)
-            go(remote(res.at[0, c, p], zin.at[dz - 1], zz_s.at[dz - 1], zz_r.at[dz - 1],
-                      q, p * 2 + c))
+        if i == 1:
+            for p in early:
+                first_leg(3, p)
+        if i == 2:
+            first_leg(1, early[0])
+    first_leg(2, early[1])
+    for p in early:
+        second_leg(p)
+    for p in late:
+        first_leg(3, p)
+    first_leg(1, late[0])
+    first_leg(2, late[1])
+    for p in early:
+        finish(p)
+    for p in late:
+        second_leg(p)
+    for p in late:
+        finish(p)
+    total = res[0, c, z].astype(jnp.float32)
     for dz in (1, 2, 3):
         remote(zin.at[dz - 1], zin.at[dz - 1], zz_s.at[0], zz_r.at[dz - 1], q, twin).wait_recv()
         total = total + zin[dz - 1].astype(jnp.float32)
     out[...] = total.astype(jnp.bfloat16)
     for cp in sends:
         cp.wait_send()
+    for p, cp in ends:
+
+        @pl.when(z != p)
+        def _():
+            cp.wait_send()
+
+    @pl.when(middle)
+    def _():
+        outward.wait_send()
+        for cp in passed:
+            cp.wait_send()
 
 
 def fused(tokens, w_gate, w_up, w_down, route_ids, route_weight):
@@ -362,10 +421,10 @@
             pltpu.VMEM((3, 2, tb, wide), bf),
             pltpu.VMEM((3, 2, tb, wide), bf),
             pltpu.VMEM((3, tb, wide), bf),
-            dma((4, 8)), dma((3,)), dma((4, 4)), dma((3,)), dma((3,)), dma((3,)),
+            dma((4, 8)), dma((5,)), dma((4, 4)), dma((3,)), dma((3,)), dma((3,)),
             dma((7,)), dma((8,)), dma((2, 2)), dma((2,)),
             dma((4, 4)), dma((4, 4)), dma((3, 2)), dma((3, 2)), dma((3, 2)), dma((3, 2)),
-            dma((3,)), dma((3,)),
+            dma((4,)), dma((3,)),
         ],
         compiler_params=pltpu.CompilerParams(
             collective_id=0, has_side_effects=True, vmem_limit_bytes=63 * 1024 * 1024

time: 151 us -> 139 us (0.921)
  Pallas kernels: 146 us -> 135 us
    pallas_call x1, Pallas kernels: 146 us -> 135 us  [fused(): pl.pallas_call(kernel, out_shape=jax.ShapeDtypeStruct((tb, wide), bf), in...]
where the time goes in v2:
time: 139 us
  Pallas kernels  135 us (97%)
  other arithmetic  1.97 us (1%)
  local copies, waits for them, and re-layouts  1.67 us (1%)
    pallas_call x1, Pallas kernels, fused(): pl.pallas_call(kernel, out_shape=jax.ShapeDtypeStruct((tb, wide), bf), in...  135 us

profile of v2, /device:TPU:0, one launch (start us, length us, event | category | flops | bytes accessed | tf_op | source)
XLA Modules:
  0.0 139.1 jit_solution(6303808757189148133)
XLA Ops:
  0.0 0.7 convert_bitcast_fusion
  0.7 1.3 pad_maximum_fusion.meta
  2.0 135.4 %moe.1 = bf16[128,1024]{1,0:T(8,128)(2,1)} custom-call(bf16[128,4096]{1,0:T(8,128)(2,1)} %toks.1, f32[16,128]{1,0:T(8,128)} %pad_maximum_fusion.meta, bf16[8,4096,384]{2,1,0:T(8,128)(2,1)} %wg.1, bf16[8,4096,384]{2,1,0:T(8,128)(2,1)} %wu.1, bf16[8,384,4096]{2,1,0:T(8,128)(2,1)} %wd.1), custom_call_target="tpu_custom_call" | custom-call | flops 20000000000 | bytes 80000000 | tf_op jit(solution)/shard_map/moe/pallas_call | solution.py:403
  137.4 1.7 %copy.8 = bf16[128,1024]{1,0:T(8,128)(2,1)} copy(bf16[128,1024]{1,0:T(8,128)(2,1)} %moe.1) | data formatting | bytes 524288
